TPU v7x, 32 devices: a whole 2x2x4 slice. The times are simulated.
32 devices in a mesh: groups: 2 (over y), rows: 2 (over x), expert: 4 (over z), pair: 2 (over core).
Axes of the slice: x: 2, y: 2, z: 4, core: 2. Of those that a mesh axis runs over, the one named last changes fastest.
Arguments:
- acts: bfloat16 [512, 6144], P(('groups', 'rows', 'expert'), 'pair'), parts along dimension 0, may hold values from -6 to 6
- grads: bfloat16 [512, 2, 16384], P(('groups', 'rows', 'expert'), None, 'pair'), parts along dimension 0, may hold values from -0.1796875 to 0.1796875
- routes: int32 [512, 2], P(('groups', 'rows', 'expert')), parts along dimension 0, may hold values from 0 to 3, all different within a row; in each aligned block of 32 rows (0 to 31, 32 to 63, ...) at most 24 rows name the same one
- seq_ids: int32 [512], P(('groups', 'rows', 'expert')), parts along dimension 0, may hold values from 0 to 3, never falling along the last dimension, each value on 1 to 96 neighbouring positions
- p_in: bfloat16 [4, 2, 3072, 64], P('expert', 'pair', 'rows'), may hold values from -0.078125 to 0.078125
- p_out: bfloat16 [4, 2, 8192, 64], P('expert', 'pair', 'rows'), may hold values from -0.046875 to 0.046875
Outputs:
- features: float32 [8, 4, 4096], P('groups', 'expert', ('rows', 'pair')), parts along dimension 0
There are 2 independent parts, one for each index of `groups`. A program takes and returns all parts, laid end to end along the dimension named above; an argument that names none is the same for every part. Nothing has to cross between parts.
Inputs may be any that keep to these rules, and one draw needn't show every extreme that they name: `routes`: in the rows of one device (aligned blocks of 32 tokens) no expert is named by more than 24 entries, and in every draw some expert is named by exactly 24 entries in some block; a token never names one expert twice. `seq_ids`: never falling along the tokens; every sequence holds 1 to 96 tokens, one exactly that many.
All inputs are finite; a program needn't handle non-finite values.
Results may differ from a plain program's by a relative error of at most 0.0003.
Values may be sent and summed in bfloat16 or wider, within the bound.
A program may use at most 64 MiB of HBM per device.

v0:
```python
import jax
import jax.numpy as jnp
from jax import lax
from jax.sharding import PartitionSpec as P

SEQS = 4


def bucket_entries(routes, n_experts, capacity):
    flat = routes.reshape(-1)
    expert_range = jnp.arange(n_experts, dtype=jnp.int32)
    member = (flat[:, None] == expert_range[None, :]).astype(jnp.int32)
    places = jnp.cumsum(member, axis=0) - 1
    place = jnp.sum(places * member, axis=1)
    slot_range = jnp.arange(capacity, dtype=jnp.int32)
    hits = member[:, :, None] * (place[:, None, None] == slot_range[None, None, :]).astype(
        jnp.int32
    )
    entry_index = jnp.arange(flat.shape[0], dtype=jnp.int32)
    source = jnp.sum(hits * entry_index[:, None, None], axis=0)
    filled = jnp.sum(hits, axis=0)
    return (source, filled)


def per_device(acts, grads, routes, seq_ids, p_in, p_out):
    tok = routes.shape[0]
    top = routes.shape[1]
    half_d = acts.shape[1]
    half_ff = grads.shape[2]
    k_in = p_in.shape[3]
    k_out = p_out.shape[3]
    feat = k_in * k_out
    n_rows = lax.axis_size("rows")
    n_exp = lax.axis_size("expert") * p_in.shape[0]
    capacity = min(tok, 3 * tok // lax.axis_size("expert"))
    d_piece = half_d // n_rows
    f_piece = half_ff // n_rows
    seq_range = jnp.arange(SEQS, dtype=jnp.int32)
    source, filled = bucket_entries(routes, n_exp, capacity)
    token_of = source // top
    keep = filled.astype(jnp.bfloat16)[:, :, None]
    a_buckets = jnp.take(acts, token_of.reshape(-1), axis=0).reshape(n_exp, capacity, half_d) * keep
    g_buckets = (
        jnp.take(grads.reshape(tok * top, half_ff), source.reshape(-1), axis=0).reshape(
            n_exp, capacity, half_ff
        )
        * keep
    )
    labels = jnp.where(
        filled == 1, jnp.take(seq_ids, token_of.reshape(-1)).reshape(n_exp, capacity), -1
    )
    a_parts = a_buckets.reshape(n_exp, capacity, n_rows, d_piece).transpose(2, 0, 1, 3)
    g_parts = g_buckets.reshape(n_exp, capacity, n_rows, f_piece).transpose(2, 0, 1, 3)
    label_parts = jnp.broadcast_to(labels.astype(jnp.bfloat16)[None], (n_rows, n_exp, capacity))
    a_recv, g_recv, label_recv = (
        lax.all_to_all(
            a_parts.reshape(n_rows * n_exp, capacity, d_piece),
            ("rows", "expert"),
            split_axis=0,
            concat_axis=0,
            tiled=True,
        ),
        lax.all_to_all(
            g_parts.reshape(n_rows * n_exp, capacity, f_piece),
            ("rows", "expert"),
            split_axis=0,
            concat_axis=0,
            tiled=True,
        ),
        lax.all_to_all(
            label_parts.reshape(n_rows * n_exp, capacity),
            ("rows", "expert"),
            split_axis=0,
            concat_axis=0,
            tiled=True,
        ),
    )
    slots = n_rows * n_exp * capacity
    a_rows = a_recv.reshape(slots, d_piece)
    g_rows = g_recv.reshape(slots, f_piece)
    slot_labels = label_recv.reshape(slots).astype(jnp.int32)
    u_part = jnp.dot(a_rows, p_in.reshape(d_piece, k_in), preferred_element_type=jnp.float32)
    v_part = jnp.dot(g_rows, p_out.reshape(f_piece, k_out), preferred_element_type=jnp.float32)
    groups = lax.axis_size(("rows", "pair"))
    share = feat // groups
    u_all, v_all = lax.psum((u_part, v_part), ("rows", "pair"))
    columns = lax.axis_index(("rows", "pair")) * share + jnp.arange(share, dtype=jnp.int32)
    u_cols = jnp.take(u_all, columns // k_out, axis=1)
    v_cols = jnp.take(v_all, columns % k_out, axis=1)
    onehot = (slot_labels[None, :] == seq_range[:, None]).astype(jnp.float32)
    block = jnp.dot(onehot, u_cols * v_cols, precision=lax.Precision.HIGHEST)
    return block.reshape(SEQS, 1, share)


def solution(mesh):
    return jax.shard_map(
        per_device,
        mesh=mesh,
        in_specs=(
            P(("groups", "rows", "expert"), "pair"),
            P(("groups", "rows", "expert"), None, "pair"),
            P(("groups", "rows", "expert"), None),
            P(("groups", "rows", "expert")),
            P("expert", "pair", "rows", None),
            P("expert", "pair", "rows", None),
        ),
        out_specs=P("groups", "expert", ("rows", "pair")),
        check_vma=False,
    )
```

profile of v0, /device:TPU:0, one launch (start us, length us, event | category | flops | bytes accessed | tf_op | source)
XLA Modules:
  0.0 132.2 jit_solution(3614667889216256828)
XLA Ops:
  6.5 0.0 copy-start
  6.5 0.0 copy-start.2
  6.5 0.8 copy.22
  7.4 0.1 eq.62
  7.5 0.1 fusion.13
  7.5 0.1 copy.23
  7.6 0.1 reduce_window_sum.11
  7.7 0.2 select_reduce_fusion
  7.9 0.2 multiply_reduce_fusion
  8.1 0.1 reduce_sum.32
  8.3 1.6 %gather_fusion = s32[96]{0:T(128)S(1)} fusion(s32[32]{0:T(128)} %param.11, s32[1024]{0:T(1024)S(1)} %get-tuple-element.16), kind=kCustom, calls=%fused_computation.2 | custom fusion | bytes 1152 | tf_op jit(solution)/shard_map/jit(_take)/gather | solution.py:50
  9.9 0.1 gather.22
  9.9 0.0 copy-done.2
  9.9 0.9 gather_fusion.1
  10.9 0.0 copy-start.3
  10.9 0.4 gather.24
  11.3 1.0 fusion.4
  12.3 7.3 %all-to-all-start.1 = ((bf16[8,24,1536]{2,1,0:T(8,128)(2,1)}), bf16[8,24,1536]{2,1,0:T(8,128)(2,1)S(1)}, u32[]{:S(2)}, u32[]{:S(2)}) async-start(bf16[8,24,1536]{2,1,0:T(8,128)(2,1)} %bitcast.3), calls=%async_computation.1 | async-start | bytes 1179648 | tf_op jit(solution)/shard_map/all_to_all | solution.py:56
  19.5 0.0 copy-done.3
  19.6 0.4 reshape.266
  20.0 2.7 %gather_fusion.2 = bf16[96,8192]{1,0:T(8,128)(2,1)} fusion(bf16[64,8192]{1,0:T(8,128)(2,1)S(1)} %reshape.266, s32[1024]{0:T(1024)S(1)} %get-tuple-element.15), kind=kCustom, calls=%fused_computation.4 | custom fusion | bytes 3146112 | tf_op jit(solution)/shard_map/jit(_take)/gather | solution.py:44
  22.7 2.9 %gather.26 = bf16[4,24,2,4096]{3,2,1,0:T(2,128)(2,1)S(1)} reshape(bf16[96,8192]{1,0:T(8,128)(2,1)} %gather_fusion.2) | data formatting | bytes 3145728 | tf_op jit(solution)/shard_map/jit(_take)/gather | solution.py:44
  25.6 3.0 %fusion = bf16[4,24,2,4096]{3,1,0,2:T(8,128)(2,1)} fusion(bf16[4,24,2,4096]{3,2,1,0:T(2,128)(2,1)S(1)} %gather.26, pred[4,24]{1,0:T(4,128)(4,1)S(1)} %compare_and_fusion.2, bf16[4,24]{1,0:T(4,128)(2,1)S(1)} %get-tuple-element.12), kind=kLoop, calls=%fused_computation.6 | loop fusion | flops 1572864 | bytes 3146016 | tf_op jit(solution)/shard_map/mul | solution.py:44
  28.6 7.8 %all-to-all-done.1 = bf16[8,24,1536]{2,1,0:T(8,128)(2,1)S(1)} async-done(((bf16[8,24,1536]{2,1,0:T(8,128)(2,1)}), bf16[8,24,1536]{2,1,0:T(8,128)(2,1)S(1)}, u32[]{:S(2)}, u32[]{:S(2)}) %all-to-all-start.1) | async-done | bytes 589856 | tf_op jit(solution)/shard_map/all_to_all | solution.py:56
  36.3 0.0 copy-start.4
  36.3 3.7 %all-to-all-start.2 = ((bf16[8,24,4096]{2,1,0:T(8,128)(2,1)}), bf16[8,24,4096]{2,1,0:T(8,128)(2,1)S(1)}, u32[]{:S(2)}, u32[]{:S(2)}) async-start(bf16[8,24,4096]{2,1,0:T(8,128)(2,1)} %bitcast.32), calls=%async_computation.2 | async-start | bytes 3145728 | tf_op jit(solution)/shard_map/all_to_all | solution.py:63
  40.1 0.6 copy.24
  40.7 0.0 copy-done.4
  40.7 0.9 fusion.10
  41.6 35.0 %all-to-all-done.2 = bf16[8,24,4096]{2,1,0:T(8,128)(2,1)S(1)} async-done(((bf16[8,24,4096]{2,1,0:T(8,128)(2,1)}), bf16[8,24,4096]{2,1,0:T(8,128)(2,1)S(1)}, u32[]{:S(2)}, u32[]{:S(2)}) %all-to-all-start.2) | async-done | bytes 1572896 | tf_op jit(solution)/shard_map/all_to_all | solution.py:63
  76.6 3.3 %all-to-all-start = ((bf16[8,1,24]{2,1,0:T(2,128)(2,1)}), bf16[8,1,24]{2,1,0:T(2,128)(2,1)S(1)}, u32[]{:S(2)}, u32[]{:S(2)}) async-start(bf16[8,1,24]{2,1,0:T(2,128)(2,1)} %copy.24), calls=%async_computation | async-start | bytes 8192 | tf_op jit(solution)/shard_map/all_to_all | solution.py:70
  80.0 0.0 all-reduce.3.cloned.1.call-start
  80.0 0.0 copy-done
  80.0 1.3 fusion.5
  81.3 0.0 all-reduce.3.cloned.1.call-update
  81.3 5.0 %all-to-all-done = bf16[8,1,24]{2,1,0:T(2,128)(2,1)S(1)} async-done(((bf16[8,1,24]{2,1,0:T(2,128)(2,1)}), bf16[8,1,24]{2,1,0:T(2,128)(2,1)S(1)}, u32[]{:S(2)}, u32[]{:S(2)}) %all-to-all-start) | async-done | bytes 416 | tf_op jit(solution)/shard_map/all_to_all | solution.py:70
  86.3 0.1 reshape.271
  86.4 29.7 %all-reduce.3.cloned.1.call-done = (f32[192,64]{0,1:T(8,128)}, f32[192,64]{0,1:T(8,128)}) async-done(((f32[192,64]{0,1:T(8,128)}, f32[192,64]{0,1:T(8,128)}), (f32[192,64]{0,1:T(8,128)}, f32[192,64]{0,1:T(8,128)})) %all-reduce.3.cloned.1.call-update) | async-done | bytes 98320 | tf_op jit(solution)/shard_map/psum | solution.py:86
  116.1 0.0 copy-start.1
  116.1 4.3 %gather_fusion.4 = f32[1024,192]{1,0:T(8,128)S(1)} fusion(f32[192,64]{0,1:T(8,128)} %get-tuple-element.8, s32[1024]{0:T(1024)S(1)} %get-tuple-element.19), kind=kCustom, calls=%fused_computation.1.clone | custom fusion | bytes 1576960 | tf_op jit(solution)/shard_map/jit(_take)/gather | solution.py:89
  120.4 0.0 copy-done.1
  120.4 3.5 %gather_fusion.3 = f32[1024,192]{1,0:T(8,128)S(1)} fusion(f32[192,64]{0,1:T(8,128)S(1)} %copy-done.1, s32[1024]{0:T(1024)S(1)} %get-tuple-element.20), kind=kCustom, calls=%fused_computation.clone | custom fusion | bytes 1576960 | tf_op jit(solution)/shard_map/jit(_take)/gather | solution.py:88
  123.9 0.8 convolution_bitcast_fusion
  124.7 0.6 copy.27
  (9 shorter events, 0.1 us)
Async XLA Ops:
  6.5 73.5 %copy-start = (bf16[1,1,4096,64]{2,3,1,0:T(8,128)(2,1)S(1)}, bf16[1,1,4096,64]{2,3,1,0:T(8,128)(2,1)}, u32[]{:S(2)}) copy-start(bf16[1,1,4096,64]{2,3,1,0:T(8,128)(2,1)} %param.13) | copy-start | bytes 1572868
  6.5 3.4 %copy-start.2 = (bf16[32,3072]{1,0:T(8,128)(2,1)S(1)}, bf16[32,3072]{1,0:T(8,128)(2,1)}, u32[]{:S(2)}) copy-start(bf16[32,3072]{1,0:T(8,128)(2,1)} %param.8) | copy-start | bytes 589828
  10.9 8.7 %copy-start.3 = (bf16[32,2,8192]{2,1,0:T(2,128)(2,1)S(1)}, bf16[32,2,8192]{2,1,0:T(2,128)(2,1)}, u32[]{:S(2)}) copy-start(bf16[32,2,8192]{2,1,0:T(2,128)(2,1)} %param.9) | copy-start | bytes 3145732
  12.3 24.0 %all-to-all-start.1 = ((bf16[8,24,1536]{2,1,0:T(8,128)(2,1)}), bf16[8,24,1536]{2,1,0:T(8,128)(2,1)S(1)}, u32[]{:S(2)}, u32[]{:S(2)}) async-start(bf16[8,24,1536]{2,1,0:T(8,128)(2,1)} %bitcast.3), calls=%async_computation.1 | async-start | bytes 1179648 | tf_op jit(solution)/shard_map/all_to_all | solution.py:56
  36.3 4.4 %copy-start.4 = (bf16[1,1,1536,64]{2,3,1,0:T(8,128)(2,1)S(1)}, bf16[1,1,1536,64]{2,3,1,0:T(8,128)(2,1)}, u32[]{:S(2)}) copy-start(bf16[1,1,1536,64]{2,3,1,0:T(8,128)(2,1)} %param.12) | copy-start | bytes 589828
  36.3 40.3 %all-to-all-start.2 = ((bf16[8,24,4096]{2,1,0:T(8,128)(2,1)}), bf16[8,24,4096]{2,1,0:T(8,128)(2,1)S(1)}, u32[]{:S(2)}, u32[]{:S(2)}) async-start(bf16[8,24,4096]{2,1,0:T(8,128)(2,1)} %bitcast.32), calls=%async_computation.2 | async-start | bytes 3145728 | tf_op jit(solution)/shard_map/all_to_all | solution.py:63
  76.6 9.6 %all-to-all-start = ((bf16[8,1,24]{2,1,0:T(2,128)(2,1)}), bf16[8,1,24]{2,1,0:T(2,128)(2,1)S(1)}, u32[]{:S(2)}, u32[]{:S(2)}) async-start(bf16[8,1,24]{2,1,0:T(2,128)(2,1)} %copy.24), calls=%async_computation | async-start | bytes 8192 | tf_op jit(solution)/shard_map/all_to_all | solution.py:70
  80.0 36.1 %all-reduce.3.cloned.1.call-start = ((), (), s32[]{:S(2)}) async-start(), calls=%async_computation.3 | async-start | bytes 262144 | tf_op jit(solution)/shard_map/psum | solution.py:86
  116.1 4.3 %copy-start.1 = (f32[192,64]{0,1:T(8,128)S(1)}, f32[192,64]{0,1:T(8,128)}, u32[]{:S(2)}) copy-start(f32[192,64]{0,1:T(8,128)} %get-tuple-element.9) | copy-start | bytes 147460
Sparse Core Ops, SparseCore 0:
  83.2 32.8 all-reduce.2
where the time goes:
time: 133 us; the launch traced here: 132 us
  waiting for transfers between devices  77.4 us (58%)
  local copies, waits for them, and re-layouts  19.2 us (14%)
  starting transfers between devices  14.3 us (11%)
  between operations  13.6 us (10%)
  other arithmetic  4.63 us (3%)
  matrix products  2.98 us (2%)
    all_to_all x1, waiting for transfers between devices, per_device(): lax.all_to_all(g_parts.reshape(n_rows * n_exp, capacity, f_piece), ('rows...  35 us
    psum x1, waiting for transfers between devices, per_device(): u_all, v_all = lax.psum((u_part, v_part), ('rows', 'pair'))  29.7 us
    all_to_all x1, waiting for transfers between devices, per_device(): lax.all_to_all(a_parts.reshape(n_rows * n_exp, capacity, d_piece), ('rows...  7.76 us
    all_to_all x1, starting transfers between devices, per_device(): lax.all_to_all(a_parts.reshape(n_rows * n_exp, capacity, d_piece), ('rows...  7.25 us
    gather x2, local copies, waits for them, and re-layouts, per_device(): jnp.take(grads.reshape(tok * top, half_ff), source.reshape(-1), axis=0)  5.56 us
    all_to_all x1, waiting for transfers between devices, per_device(): lax.all_to_all(label_parts.reshape(n_rows * n_exp, capacity), ('rows', 'e...  4.98 us
    gather x1, local copies, waits for them, and re-layouts, per_device(): v_cols = jnp.take(v_all, columns % k_out, axis=1)  4.33 us
    all_to_all x1, starting transfers between devices, per_device(): lax.all_to_all(g_parts.reshape(n_rows * n_exp, capacity, f_piece), ('rows...  3.71 us
  transfers between devices with their start and end apart: 4, of which 4 were waited for; matrix products, arithmetic and copies ran while one was open for 9% of the time, Pallas kernels for 0%

commit v1 on v0

--- a/solution.py
+++ b/solution.py
@@ -2,6 +2,7 @@
 import jax.numpy as jnp
 from jax import lax
 from jax.sharding import PartitionSpec as P
+from jax.lax import psum
 
 SEQS = 4
 
@@ -83,7 +84,8 @@
     v_part = jnp.dot(g_rows, p_out.reshape(f_piece, k_out), preferred_element_type=jnp.float32)
     groups = lax.axis_size(("rows", "pair"))
     share = feat // groups
-    u_all, v_all = lax.psum((u_part, v_part), ("rows", "pair"))
+    place_leaf = lambda load: psum(psum(load, "pair"), "rows")
+    u_all, v_all = place_leaf((u_part, v_part))
     columns = lax.axis_index(("rows", "pair")) * share + jnp.arange(share, dtype=jnp.int32)
     u_cols = jnp.take(u_all, columns // k_out, axis=1)
     v_cols = jnp.take(v_all, columns % k_out, axis=1)

time: 133 us -> 144 us (1.083)
  waiting for transfers between devices: 77.4 us -> 88.9 us
    psum x1 -> x2, waiting for transfers between devices: 29.7 us -> 46.1 us  [per_device(): place_leaf = lambda load: psum(psum(load, 'pair'), 'rows')]
    all_to_all x1, waiting for transfers between devices: 4.98 us -> 0.01 us  [per_device(): lax.all_to_all(label_parts.reshape(n_rows * n_exp, capacity), ('rows', 'e...]
  transfers between devices with their start and end apart: 4 -> 5, of which waited for: 4 -> 4; matrix products, arithmetic and copies ran while one was open for 9% -> 8% of each run, Pallas kernels for 0% -> 0%
where the time goes in v1:
time: 144 us
  waiting for transfers between devices  88.9 us (62%)
  local copies, waits for them, and re-layouts  19.2 us (13%)
  starting transfers between devices  14.4 us (10%)
  between operations  13.6 us (9%)
  other arithmetic  4.63 us (3%)
  matrix products  2.98 us (2%)
    psum x2, waiting for transfers between devices, per_device(): place_leaf = lambda load: psum(psum(load, 'pair'), 'rows')  46.1 us
    all_to_all x1, waiting for transfers between devices, per_device(): lax.all_to_all(g_parts.reshape(n_rows * n_exp, capacity, f_piece), ('rows...  35 us
    all_to_all x1, waiting for transfers between devices, per_device(): lax.all_to_all(a_parts.reshape(n_rows * n_exp, capacity, d_piece), ('rows...  7.78 us
    all_to_all x1, starting transfers between devices, per_device(): lax.all_to_all(a_parts.reshape(n_rows * n_exp, capacity, d_piece), ('rows...  7.25 us
    gather x2, local copies, waits for them, and re-layouts, per_device(): jnp.take(grads.reshape(tok * top, half_ff), source.reshape(-1), axis=0)  5.55 us
    gather x1, local copies, waits for them, and re-layouts, per_device(): v_cols = jnp.take(v_all, columns % k_out, axis=1)  4.33 us
    all_to_all x1, starting transfers between devices, per_device(): lax.all_to_all(g_parts.reshape(n_rows * n_exp, capacity, f_piece), ('rows...  3.71 us
    gather x1, local copies, waits for them, and re-layouts, per_device(): u_cols = jnp.take(u_all, columns // k_out, axis=1)  3.47 us
  transfers between devices with their start and end apart: 5, of which 4 were waited for; matrix products, arithmetic and copies ran while one was open for 8% of the time, Pallas kernels for 0%

profile of v1, /device:TPU:0, one launch (start us, length us, event | category | flops | bytes accessed | tf_op | source)
XLA Modules:
  0.0 143.7 jit_solution(12240648069070171379)
XLA Ops:
  6.5 0.0 copy-start
  6.5 0.0 copy-start.2
  6.5 0.8 copy.22
  7.4 0.1 eq.62
  7.5 0.1 fusion.13
  7.5 0.1 copy.23
  7.6 0.1 reduce_window_sum.11
  7.7 0.2 select_reduce_fusion
  7.9 0.2 multiply_reduce_fusion
  8.1 0.1 reduce_sum.32
  8.3 1.6 %gather_fusion = s32[96]{0:T(128)S(1)} fusion(s32[32]{0:T(128)} %param.11, s32[1024]{0:T(1024)S(1)} %get-tuple-element.18), kind=kCustom, calls=%fused_computation.2 | custom fusion | bytes 1152 | tf_op jit(solution)/shard_map/jit(_take)/gather | solution.py:51
  9.9 0.1 gather.22
  9.9 0.0 copy-done.2
  9.9 0.9 gather_fusion.1
  10.9 0.0 copy-start.3
  10.9 0.4 gather.24
  11.3 1.0 fusion.4
  12.3 7.3 %all-to-all-start.1 = ((bf16[8,24,1536]{2,1,0:T(8,128)(2,1)}), bf16[8,24,1536]{2,1,0:T(8,128)(2,1)S(1)}, u32[]{:S(2)}, u32[]{:S(2)}) async-start(bf16[8,24,1536]{2,1,0:T(8,128)(2,1)} %bitcast.3), calls=%async_computation.1 | async-start | bytes 1179648 | tf_op jit(solution)/shard_map/all_to_all | solution.py:57
  19.6 0.0 copy-done.3
  19.6 0.4 reshape.266
  20.0 2.7 %gather_fusion.2 = bf16[96,8192]{1,0:T(8,128)(2,1)} fusion(bf16[64,8192]{1,0:T(8,128)(2,1)S(1)} %reshape.266, s32[1024]{0:T(1024)S(1)} %get-tuple-element.17), kind=kCustom, calls=%fused_computation.4 | custom fusion | bytes 3146112 | tf_op jit(solution)/shard_map/jit(_take)/gather | solution.py:45
  22.7 2.9 %gather.26 = bf16[4,24,2,4096]{3,2,1,0:T(2,128)(2,1)S(1)} reshape(bf16[96,8192]{1,0:T(8,128)(2,1)} %gather_fusion.2) | data formatting | bytes 3145728 | tf_op jit(solution)/shard_map/jit(_take)/gather | solution.py:45
  25.6 3.0 %fusion = bf16[4,24,2,4096]{3,1,0,2:T(8,128)(2,1)} fusion(bf16[4,24,2,4096]{3,2,1,0:T(2,128)(2,1)S(1)} %gather.26, pred[4,24]{1,0:T(4,128)(4,1)S(1)} %compare_and_fusion.2, bf16[4,24]{1,0:T(4,128)(2,1)S(1)} %get-tuple-element.14), kind=kLoop, calls=%fused_computation.6 | loop fusion | flops 1572864 | bytes 3146016 | tf_op jit(solution)/shard_map/mul | solution.py:45
  28.6 7.8 %all-to-all-done.1 = bf16[8,24,1536]{2,1,0:T(8,128)(2,1)S(1)} async-done(((bf16[8,24,1536]{2,1,0:T(8,128)(2,1)}), bf16[8,24,1536]{2,1,0:T(8,128)(2,1)S(1)}, u32[]{:S(2)}, u32[]{:S(2)}) %all-to-all-start.1) | async-done | bytes 589856 | tf_op jit(solution)/shard_map/all_to_all | solution.py:57
  36.3 0.0 copy-start.4
  36.3 3.7 %all-to-all-start.2 = ((bf16[8,24,4096]{2,1,0:T(8,128)(2,1)}), bf16[8,24,4096]{2,1,0:T(8,128)(2,1)S(1)}, u32[]{:S(2)}, u32[]{:S(2)}) async-start(bf16[8,24,4096]{2,1,0:T(8,128)(2,1)} %bitcast.32), calls=%async_computation.2 | async-start | bytes 3145728 | tf_op jit(solution)/shard_map/all_to_all | solution.py:64
  40.1 0.6 copy.24
  40.7 0.0 copy-done.4
  40.7 0.9 fusion.10
  41.6 35.0 %all-to-all-done.2 = bf16[8,24,4096]{2,1,0:T(8,128)(2,1)S(1)} async-done(((bf16[8,24,4096]{2,1,0:T(8,128)(2,1)}), bf16[8,24,4096]{2,1,0:T(8,128)(2,1)S(1)}, u32[]{:S(2)}, u32[]{:S(2)}) %all-to-all-start.2) | async-done | bytes 1572896 | tf_op jit(solution)/shard_map/all_to_all | solution.py:64
  76.6 3.3 %all-to-all-start = ((bf16[8,1,24]{2,1,0:T(2,128)(2,1)}), bf16[8,1,24]{2,1,0:T(2,128)(2,1)S(1)}, u32[]{:S(2)}, u32[]{:S(2)}) async-start(bf16[8,1,24]{2,1,0:T(2,128)(2,1)} %copy.24), calls=%async_computation | async-start | bytes 8192 | tf_op jit(solution)/shard_map/all_to_all | solution.py:71
  80.0 0.0 all-reduce.5.cloned.1.call-start
  80.0 0.0 copy-done
  80.0 1.2 fusion.5
  81.3 0.0 all-reduce.5.cloned.1.call-update
  81.3 0.0 all-reduce.7.cloned.1.call-start
  81.4 21.2 %all-reduce.5.cloned.1.call-done = (f32[192,64]{0,1:T(8,128)}, f32[192,64]{0,1:T(8,128)}) async-done(((f32[192,64]{0,1:T(8,128)}, f32[192,64]{0,1:T(8,128)}), (f32[192,64]{0,1:T(8,128)}, f32[192,64]{0,1:T(8,128)})) %all-reduce.5.cloned.1.call-update) | async-done | bytes 98320 | tf_op jit(solution)/shard_map/psum | solution.py:87
  102.5 0.0 all-reduce.7.cloned.1.call-update
  102.5 0.0 all-to-all-done
  102.6 0.1 reshape.271
  102.7 25.0 %all-reduce.7.cloned.1.call-done = (f32[192,64]{0,1:T(8,128)}, f32[192,64]{0,1:T(8,128)}) async-done(((f32[192,64]{0,1:T(8,128)}, f32[192,64]{0,1:T(8,128)}), (f32[192,64]{0,1:T(8,128)}, f32[192,64]{0,1:T(8,128)})) %all-reduce.7.cloned.1.call-update) | async-done | bytes 98320 | tf_op jit(solution)/shard_map/psum | solution.py:87
  127.6 0.0 copy-start.1
  127.6 4.3 %gather_fusion.4 = f32[1024,192]{1,0:T(8,128)S(1)} fusion(f32[192,64]{0,1:T(8,128)} %get-tuple-element.10, s32[1024]{0:T(1024)S(1)} %get-tuple-element.21), kind=kCustom, calls=%fused_computation.1.clone | custom fusion | bytes 1576960 | tf_op jit(solution)/shard_map/jit(_take)/gather | solution.py:91
  132.0 0.0 copy-done.1
  132.0 3.5 %gather_fusion.3 = f32[1024,192]{1,0:T(8,128)S(1)} fusion(f32[192,64]{0,1:T(8,128)S(1)} %copy-done.1, s32[1024]{0:T(1024)S(1)} %get-tuple-element.22), kind=kCustom, calls=%fused_computation.clone | custom fusion | bytes 1576960 | tf_op jit(solution)/shard_map/jit(_take)/gather | solution.py:90
  135.4 0.8 convolution_bitcast_fusion
  136.2 0.6 copy.27
  (9 shorter events, 0.1 us)
Async XLA Ops:
  6.5 73.5 %copy-start = (bf16[1,1,4096,64]{2,3,1,0:T(8,128)(2,1)S(1)}, bf16[1,1,4096,64]{2,3,1,0:T(8,128)(2,1)}, u32[]{:S(2)}) copy-start(bf16[1,1,4096,64]{2,3,1,0:T(8,128)(2,1)} %param.13) | copy-start | bytes 1572868
  6.5 3.4 %copy-start.2 = (bf16[32,3072]{1,0:T(8,128)(2,1)S(1)}, bf16[32,3072]{1,0:T(8,128)(2,1)}, u32[]{:S(2)}) copy-start(bf16[32,3072]{1,0:T(8,128)(2,1)} %param.8) | copy-start | bytes 589828
  10.9 8.7 %copy-start.3 = (bf16[32,2,8192]{2,1,0:T(2,128)(2,1)S(1)}, bf16[32,2,8192]{2,1,0:T(2,128)(2,1)}, u32[]{:S(2)}) copy-start(bf16[32,2,8192]{2,1,0:T(2,128)(2,1)} %param.9) | copy-start | bytes 3145732
  12.3 24.0 %all-to-all-start.1 = ((bf16[8,24,1536]{2,1,0:T(8,128)(2,1)}), bf16[8,24,1536]{2,1,0:T(8,128)(2,1)S(1)}, u32[]{:S(2)}, u32[]{:S(2)}) async-start(bf16[8,24,1536]{2,1,0:T(8,128)(2,1)} %bitcast.3), calls=%async_computation.1 | async-start | bytes 1179648 | tf_op jit(solution)/shard_map/all_to_all | solution.py:57
  36.3 4.4 %copy-start.4 = (bf16[1,1,1536,64]{2,3,1,0:T(8,128)(2,1)S(1)}, bf16[1,1,1536,64]{2,3,1,0:T(8,128)(2,1)}, u32[]{:S(2)}) copy-start(bf16[1,1,1536,64]{2,3,1,0:T(8,128)(2,1)} %param.12) | copy-start | bytes 589828
  36.3 40.3 %all-to-all-start.2 = ((bf16[8,24,4096]{2,1,0:T(8,128)(2,1)}), bf16[8,24,4096]{2,1,0:T(8,128)(2,1)S(1)}, u32[]{:S(2)}, u32[]{:S(2)}) async-start(bf16[8,24,4096]{2,1,0:T(8,128)(2,1)} %bitcast.32), calls=%async_computation.2 | async-start | bytes 3145728 | tf_op jit(solution)/shard_map/all_to_all | solution.py:64
  76.6 25.9 %all-to-all-start = ((bf16[8,1,24]{2,1,0:T(2,128)(2,1)}), bf16[8,1,24]{2,1,0:T(2,128)(2,1)S(1)}, u32[]{:S(2)}, u32[]{:S(2)}) async-start(bf16[8,1,24]{2,1,0:T(2,128)(2,1)} %copy.24), calls=%async_computation | async-start | bytes 8192 | tf_op jit(solution)/shard_map/all_to_all | solution.py:71
  80.0 22.6 %all-reduce.5.cloned.1.call-start = ((), (), s32[]{:S(2)}) async-start(), calls=%async_computation.3 | async-start | bytes 262144 | tf_op jit(solution)/shard_map/psum | solution.py:87
  81.3 46.3 %all-reduce.7.cloned.1.call-start = ((), (), s32[]{:S(2)}) async-start(), calls=%async_computation.4 | async-start | bytes 262144 | tf_op jit(solution)/shard_map/psum | solution.py:87
  127.6 4.3 %copy-start.1 = (f32[192,64]{0,1:T(8,128)S(1)}, f32[192,64]{0,1:T(8,128)}, u32[]{:S(2)}) copy-start(f32[192,64]{0,1:T(8,128)} %get-tuple-element.11) | copy-start | bytes 147460
Sparse Core Ops, SparseCore 0:
  83.1 19.3 all-reduce.4
  104.8 22.7 all-reduce.6
